TPU v7x, 256 devices: a whole 4x4x8 slice. The times are simulated.
256 devices in a mesh: stn: 64 (over z, y_hi, x), chan: 4 (over y_lo, core).
Axes of the slice: x: 4, y: 4 (y_hi: 2, y_lo: 2; y = y_hi * 2 + y_lo), z: 8, core: 2. Of those that a mesh axis runs over, the one named last changes fastest.
Arguments:
- samples: bfloat16 [512, 17, 2, 8192], P(('stn', 'chan')), may hold values from -6 to 6
- keeper: int32 [64, 64], replicated, may hold values from 0 to 1, as said below
Outputs:
- visibilities: bfloat16 [512, 2, 4096, 264], P('stn', None, 'chan')
Inputs may be any that keep to these rules, and one draw needn't show every extreme that they name: keeper[g, g] is 1; for g != h with d = (g - h) mod 64: keeper[g, h] is 1 where 0 < d < 32, 0 where d > 32, and at d = 32 exactly one of keeper[g, h] and keeper[h, g] is 1, which one drawn for each such pair; half of the rows hold 33 ones, the others 33 - 1.
All inputs are finite; a program needn't handle non-finite values.
Results may differ from a plain program's by a relative error of at most 0.0077.
Values may be sent and summed in bfloat16 or wider, within the bound.
No kernel may reach another device: no remote copies, remote signals or barrier semaphores. Data moves between devices by JAX's collectives and lax.ppermute only.
A program may use at most 192 MiB of HBM per device.

v0:
```python
import math
import jax
import jax.numpy as jnp
from jax import lax
from jax.sharding import PartitionSpec as P

NFFT = 8192
TAPS = 16
CH_WIN = 1024
DFT_BLOCK = 256


def taps_table():
    pos = jnp.arange(TAPS * NFFT).astype(jnp.float32)
    shifted = (pos + 0.5) / NFFT - TAPS / 2.0
    window = 0.5 - 0.5 * jnp.cos(2.0 * math.pi * (pos + 0.5) / (TAPS * NFFT))
    return (jnp.sinc(shifted) * window).reshape(TAPS, NFFT)


def twiddles(width):
    index_n = jnp.arange(NFFT, dtype=jnp.int32)[:, None]
    index_k = jnp.arange(width, dtype=jnp.int32)[None, :]
    phase = (index_n * index_k % NFFT).astype(jnp.float32) * (2.0 * math.pi / NFFT)
    cosines = jnp.cos(phase).astype(jnp.bfloat16)
    sines = jnp.sin(phase).astype(jnp.bfloat16)
    upper = jnp.concatenate([cosines, -sines], axis=1)
    lower = jnp.concatenate([sines, cosines], axis=1)
    return jnp.concatenate([upper, lower], axis=0)


def rotations(ch_tot, width):
    blocks = ch_tot // width
    index_n = jnp.arange(NFFT, dtype=jnp.int32)[None, :]
    index_b = jnp.arange(blocks, dtype=jnp.int32)[:, None]
    phase = (index_n * index_b * width % NFFT).astype(jnp.float32) * (2.0 * math.pi / NFFT)
    return (jnp.cos(phase), jnp.sin(phase))


def channelise(block, taps, table, cos_rot, sin_rot, ch_tot):
    frames = block.shape[1] - TAPS + 1
    count = block.shape[0]
    width = table.shape[1] // 2
    blocks = ch_tot // width
    total = taps[0] * block[:, 0:frames].astype(jnp.float32)
    for tap in range(1, TAPS):
        total = total + taps[tap] * block[:, tap : tap + frames].astype(jnp.float32)
    real_part = total[:, :, 0][None]
    imag_part = total[:, :, 1][None]
    cosine = cos_rot[:, None, None, :]
    sine = sin_rot[:, None, None, :]
    rot_real = real_part * cosine + imag_part * sine
    rot_imag = imag_part * cosine - real_part * sine
    lhs = jnp.stack([rot_real, rot_imag], axis=3).astype(jnp.bfloat16)
    lhs = lhs.reshape(blocks * count * frames, 2 * NFFT)
    spectrum = jnp.dot(lhs, table, preferred_element_type=jnp.float32) * (1.0 / math.sqrt(NFFT))
    spectrum = spectrum.astype(jnp.bfloat16).reshape(blocks, count, frames, 2, width)
    spectrum = jnp.transpose(spectrum, (1, 0, 4, 3, 2))
    return spectrum.reshape(count, ch_tot, 2, frames)


def correlate(own, others, frames):
    half = others.shape[2] // 2
    turned = jnp.concatenate([-others[:, :, half:], others[:, :, :half]], axis=2)
    rhs = jnp.concatenate([others, turned], axis=0)
    product = lax.dot_general(
        own, rhs, (((2,), (2,)), ((1,), (1,))), preferred_element_type=jnp.float32
    )
    rows = others.shape[0]
    product = product.reshape(product.shape[0], product.shape[1], 2, rows)
    return jnp.transpose(product, (1, 2, 0, 3)) / frames


def slot_table(keep_rows, keep_slots):
    ranking = jnp.cumsum(keep_rows, axis=1) - 1
    slot_index = jnp.arange(keep_slots, dtype=jnp.int32)
    matched = (keep_rows[:, :, None] == 1) & (ranking[:, :, None] == slot_index[None, None, :])
    column_ids = jnp.arange(keep_rows.shape[1], dtype=jnp.int32)
    slot_column = jnp.sum(jnp.where(matched, column_ids[None, :, None], 0), axis=1)
    filled = jnp.any(matched, axis=1)
    return (slot_column, filled)


def per_device(samples, keeper):
    n_chan = lax.axis_size("chan")
    n_stn = lax.axis_size("stn")
    ch_tot = CH_WIN * n_chan
    frames = samples.shape[1] - TAPS + 1
    cos_rot, sin_rot = rotations(ch_tot, DFT_BLOCK)
    spectrum = channelise(samples, taps_table(), twiddles(DFT_BLOCK), cos_rot, sin_rot, ch_tot)
    local = lax.all_to_all(spectrum, "chan", split_axis=1, concat_axis=0, tiled=True)
    group_in = local.shape[0]
    own = local.reshape(group_in, CH_WIN, 2 * frames)
    keep_slots = n_stn // 2 + 1
    group_index = lax.axis_index("stn")
    row_keep = jnp.take(keeper, group_index, axis=0)
    slot_column, filled = slot_table(row_keep[None], keep_slots)
    slot_column = slot_column[0]
    filled = filled[0]
    nothing = jnp.zeros((), jnp.bfloat16)
    col_mask = jnp.repeat(row_keep, group_in).astype(jnp.float32)
    tile = correlate(own, lax.all_gather(own, "stn", axis=0, tiled=True), frames)
    whole = (tile * col_mask[None, None, None, :]).astype(jnp.bfloat16)
    whole = whole.reshape(group_in, 2, CH_WIN, n_stn, group_in)
    picked = jnp.take(whole, slot_column, axis=3)
    picked = jnp.where(filled[None, None, None, :, None], picked, nothing)
    return picked.reshape(group_in, 2, CH_WIN, keep_slots * group_in)


def solution(mesh):
    placed = (P(("stn", "chan"), None, None, None), P())
    return jax.shard_map(
        per_device,
        mesh=mesh,
        in_specs=placed,
        out_specs=P("stn", None, "chan", None),
        check_vma=False,
    )
```

profile of v0, /device:TPU:2, one launch (start us, length us, event | category | flops | bytes accessed | tf_op | source)
XLA Modules:
  0.0 386.7 jit_solution(5526646558050877336)
XLA Ops:
  6.5 0.0 copy-start.1
  6.5 0.0 all-gather.2.cloned.1.call-start
  6.5 2.4 fusion.33
  8.9 2.1 fusion.45
  11.0 35.0 %sine_convert_fusion = (bf16[8192,256]{1,0:T(8,128)(2,1)}, bf16[8192,256]{1,0:T(8,128)(2,1)}) fusion(), kind=kLoop, calls=%fused_computation.25 | loop fusion | flops 33554432 | bytes 8388608 | tf_op jit(solution)/shard_map/convert_element_type | solution.py:25
  46.0 32.4 %fusion.22 = bf16[8192,256]{1,0:T(8,128)(2,1)} fusion(), kind=kLoop, calls=%fused_computation.34 | loop fusion | flops 37748736 | bytes 4194304 | tf_op jit(solution)/shard_map/neg | solution.py:26
  78.4 0.0 copy-done.1
  78.4 2.1 multiply_add_fusion.1
  80.6 0.2 fusion.52
  80.8 0.2 copy_bitcast_fusion
  81.0 4.4 %add_convert_fusion = (bf16[16,2,2,1,8192]{4,3,2,1,0:T(2,128)(2,1)S(1)}, bf16[16,2,2,1,8192]{4,3,2,1,0:T(2,128)(2,1)S(1)}) fusion(f32[16,8192]{1,0:T(8,128)S(1)} %get-tuple-element.42, f32[2,2,8192]{2,1,0:T(2,128)S(1)} %get-tuple-element.40, f32[16,8192]{1,0:T(8,128)S(1)} %get-tuple-element.43, f32[2,2,8192]{2,1,0:T(2,128)S(1)} %get-tuple-element.41), kind=kLoop, calls=%fused_computation.33 | loop fusion | flops 4194304 | bytes 3407872 | tf_op jit(solution)/shard_map/convert
  85.4 4.8 %pad_maximum_fusion = bf16[16,2,2,2,8192]{4,3,2,1,0:T(2,128)(2,1)S(1)} fusion(bf16[16,2,2,1,8192]{4,3,2,1,0:T(2,128)(2,1)S(1)} %get-tuple-element.21, bf16[16,2,2,1,8192]{4,3,2,1,0:T(2,128)(2,1)S(1)} %get-tuple-element.20), kind=kLoop, calls=%fused_computation.31 | loop fusion | flops 4194304 | bytes 4194304 | tf_op jit(solution)/shard_map/stack | solution.py:53
  90.2 1.2 copy.51
  91.4 13.7 %fusion.26 = bf16[64,512]{1,0:T(8,128)(2,1)S(1)} fusion(bf16[64,16384]{1,0:T(8,128)(2,1)S(1)} %bitcast.44, bf16[8192,256]{1,0:T(8,128)(2,1)} %get-tuple-element.45, bf16[8192,256]{1,0:T(8,128)(2,1)} %get-tuple-element.44, bf16[8192,256]{1,0:T(8,128)(2,1)} %fusion.22), kind=kOutput, calls=%fused_computation.36 | convolution fusion | flops 1140916224 | bytes 14745600 | tf_op jit(solution)/shard_map/dot_general | solution.py:55
  105.2 4.8 %copy.46 = bf16[2,16,256,2,2]{4,3,0,2,1:T(2,128)(2,1)} copy(bf16[2,16,256,2,2]{2,1,4,3,0:T(8,128)(2,1)S(1)} %bitcast.45) | data formatting | bytes 131072 | tf_op jit(solution)/shard_map/reshape | solution.py:58
  110.0 7.2 %reshape.361 = bf16[4,2,4096]{2,1,0:T(2,128)(2,1)S(1)} reshape(bf16[4096,2,2,2]{3,2,1,0:T(2,128)(2,1)} %bitcast.41) | data formatting | bytes 131072
  117.2 6.8 %all_to_all.15 = bf16[4,2,4096]{2,1,0:T(2,128)(2,1)S(1)} all-to-all(bf16[4,2,4096]{2,1,0:T(2,128)(2,1)S(1)} %reshape.361), channel_id=1, replica_groups=mesh['stn'=64,'chan'=4] {'chan'}, dimensions={0} | all-to-all | bytes 131072 | tf_op jit(solution)/shard_map/all_to_all | solution.py:90
  123.9 10.0 %reshape.362 = bf16[4096,2,2,2]{3,2,1,0:T(2,128)(2,1)} reshape(bf16[4,2,4096]{2,1,0:T(2,128)(2,1)S(1)} %all_to_all.15) | data formatting | bytes 131072
  133.9 9.7 %copy.47 = bf16[2,4,1024,2,2]{2,1,4,3,0:T(4,128)(2,1)S(1)} copy(bf16[2,4,1024,2,2]{4,3,0,2,1:T(2,128)(2,1)} %bitcast.42) | data formatting | bytes 131072 | tf_op jit(solution)/shard_map/all_to_all | solution.py:90
  143.7 0.1 copy.37
  143.8 0.7 copy.38
  144.5 0.0 all-gather.2.cloned.1.call-update
  144.5 0.7 compare_bitcast_fusion
  145.2 0.1 broadcast_in_dim.84
  145.3 0.1 mul.838
  145.4 0.1 copy.32
  145.5 0.1 reduce-window.7
  145.6 0.1 add_reduce_fusion
  145.7 0.7 select_reduce_fusion
  146.4 0.1 broadcast_in_dim.81
  146.5 0.6 broadcast_in_dim.82
  147.1 0.7 fusion.47
  147.8 0.1 broadcast_in_dim.76
  147.9 0.7 broadcast_in_dim.77
  148.6 0.7 copy.42
  149.3 125.9 %all-gather.2.cloned.1.call-done = bf16[512,1024,4]{1,2,0:T(4,128)(2,1)} async-done(((bf16[8,1024,4]{1,2,0:T(4,128)(2,1)}), bf16[512,1024,4]{1,2,0:T(4,128)(2,1)}) %all-gather.2.cloned.1.call-update) | async-done | bytes 4194320 | tf_op jit(solution)/shard_map/all_gather | solution.py:101
  275.2 10.1 %copy.41 = bf16[512,1024,4]{0,2,1:T(4,128)(2,1)} copy(bf16[512,1024,4]{1,2,0:T(4,128)(2,1)} %all-gather.2.cloned.1.call-done) | data formatting | bytes 8388608 | tf_op jit(solution)/shard_map/all_gather | solution.py:101
  285.3 0.0 copy-start
  285.3 7.7 %slice_negate_fusion = (bf16[512,1024,2]{0,2,1:T(2,128)(2,1)S(1)}, bf16[512,1024,2]{0,2,1:T(2,128)(2,1)S(1)}) fusion(bf16[512,1024,4]{0,2,1:T(4,128)(2,1)} %copy.41), kind=kLoop, calls=%fused_computation.30 | loop fusion | flops 1048576 | bytes 8388608 | tf_op jit(solution)/shard_map/neg | solution.py:63
  293.1 0.0 copy-done
  293.1 13.0 %fusion.13 = f32[1024,8,1024]{2,1,0:T(8,128)} fusion(bf16[8,1024,4]{0,2,1:T(4,128)(2,1)S(1)} %copy.42, bf16[512,1024,2]{0,2,1:T(2,128)(2,1)S(1)} %get-tuple-element.19, bf16[512,1024,2]{0,2,1:T(2,128)(2,1)S(1)} %get-tuple-element.18, bf16[512,1024,4]{0,2,1:T(4,128)(2,1)S(1)} %copy-done), kind=kOutput, calls=%fused_computation.19 | convolution fusion | flops 92274688 | bytes 42008576 | tf_op jit(solution)/shard_map/dot_general | solution.py:65
  306.1 32.2 %copy.43 = f32[1024,8,2,512]{0,3,2,1:T(8,128)} copy(f32[1024,8,2,512]{3,1,2,0:T(8,128)} %bitcast.40) | data formatting | bytes 67108864 | tf_op jit(solution)/shard_map/reshape | solution.py:69
  338.3 13.4 %fusion = bf16[8,2,1024,64,8]{2,4,3,1,0:T(8,128)(2,1)S(1)} fusion(f32[1024,8,2,512]{0,3,2,1:T(8,128)} %copy.43, f32[512]{0:T(512)S(1)} %mul.838), kind=kLoop, calls=%fused_computation.2 | loop fusion | flops 16777216 | bytes 50333696 | tf_op jit(solution)/shard_map/reshape | solution.py:103
  351.7 7.0 %copy.44 = bf16[8,2,1024,64,8]{2,4,1,0,3:T(8,128)(2,1)} copy(bf16[8,2,1024,64,8]{2,4,3,1,0:T(8,128)(2,1)S(1)} %fusion) | data formatting | bytes 33554432 | tf_op jit(solution)/shard_map/reshape | solution.py:103
  358.7 0.0 copy-start.2
  358.7 0.0 copy-start.3
  358.7 10.9 %gather_fusion = bf16[33,8,2,1024,8]{3,4,2,1,0:T(8,128)(2,1)} fusion(bf16[8,2,1024,64,8]{2,4,1,0,3:T(8,128)(2,1)} %copy.44, s32[1024]{0:T(1024)S(1)} %pad_clamp_fusion), kind=kCustom, calls=%fused_computation | custom fusion | bytes 17301636 | tf_op jit(solution)/shard_map/jit(_take)/gather | solution.py:104
  369.6 0.0 copy-done.2
  369.6 0.0 copy-done.3
  369.6 10.3 %fusion.9 = bf16[8,2,1024,264]{2,3,1,0:T(8,128)(2,1)} fusion(pred[264]{0:T(512)(128)(4,1)S(1)} %copy-done.2, pred[264]{0:T(512)(128)(4,1)S(1)} %copy-done.3, bf16[33,8,2,1024,8]{3,4,2,1,0:T(8,128)(2,1)} %gather_fusion), kind=kLoop, calls=%fused_computation.15 | loop fusion | flops 8650752 | bytes 17302032 | tf_op jit(solution)/shard_map/jit(_where)/select_n | solution.py:105
  (8 shorter events, 0.1 us)
Async XLA Ops:
  6.5 71.9 %copy-start.1 = (bf16[2,17,2,8192]{3,2,1,0:T(2,128)(2,1)S(1)}, bf16[2,17,2,8192]{3,2,1,0:T(2,128)(2,1)}, u32[]{:S(2)}) copy-start(bf16[2,17,2,8192]{3,2,1,0:T(2,128)(2,1)} %param.2) | copy-start | bytes 3342340
  6.5 268.7 %all-gather.2.cloned.1.call-start = ((), (), s32[]{:S(2)}) async-start(), calls=%async_computation.1 | async-start | bytes 4259840 | tf_op jit(solution)/shard_map/all_gather | solution.py:101
  285.3 7.8 %copy-start = (bf16[512,1024,4]{0,2,1:T(4,128)(2,1)S(1)}, bf16[512,1024,4]{0,2,1:T(4,128)(2,1)}, u32[]{:S(2)}) copy-start(bf16[512,1024,4]{0,2,1:T(4,128)(2,1)} %copy.41) | copy-start | bytes 12582916
  358.7 10.9 %copy-start.2 = (pred[264]{0:T(512)(128)(4,1)S(1)}, pred[264]{0:T(512)(128)(4,1)}, u32[]{:S(2)}) copy-start(pred[264]{0:T(512)(128)(4,1)} %broadcast_in_dim.82) | copy-start | bytes 796
  358.7 10.9 %copy-start.3 = (pred[264]{0:T(512)(128)(4,1)S(1)}, pred[264]{0:T(512)(128)(4,1)}, u32[]{:S(2)}) copy-start(pred[264]{0:T(512)(128)(4,1)} %broadcast_in_dim.77) | copy-start | bytes 796
Sparse Core Ops, SparseCore 0:
  144.6 130.5 all-gather.1
where the time goes:
time: 388 us; the launch traced here: 387 us
  waiting for transfers between devices  126 us (32%)
  other arithmetic  117 us (30%)
  local copies, waits for them, and re-layouts  96.8 us (25%)
  matrix products  26.7 us (7%)
  between operations  13.6 us (4%)
  blocking collectives  6.77 us (2%)
    all_gather x1, waiting for transfers between devices, per_device(): lax.all_gather(own, 'stn', axis=0, tiled=True)  126 us
    convert_element_type x1, other arithmetic, twiddles(): sines = jnp.sin(phase).astype(jnp.bfloat16)  35 us
    neg x1, other arithmetic, twiddles(): upper = jnp.concatenate([cosines, -sines], axis=1)  32.4 us
    reshape x1, local copies, waits for them, and re-layouts, correlate(): product = product.reshape(product.shape[0], product.shape[1], 2, rows)  32.2 us
    unnamed x12, local copies, waits for them, and re-layouts  18.6 us
    dot_general x1, matrix products, channelise(): jnp.dot(lhs, table, preferred_element_type=jnp.float32)  13.7 us
    reshape x1, other arithmetic, per_device(): whole = whole.reshape(group_in, 2, CH_WIN, n_stn, group_in)  13.4 us
    dot_general x1, matrix products, correlate(): lax.dot_general(own, rhs, (((2,), (2,)), ((1,), (1,))), preferred_element...  13 us
  transfers between devices with their start and end apart: 1, of which 1 were waited for; matrix products, arithmetic and copies ran while one was open for 1% of the time, Pallas kernels for 0%

commit v1 on v0

--- a/solution.py
+++ b/solution.py
@@ -87,7 +87,10 @@
     frames = samples.shape[1] - TAPS + 1
     cos_rot, sin_rot = rotations(ch_tot, DFT_BLOCK)
     spectrum = channelise(samples, taps_table(), twiddles(DFT_BLOCK), cos_rot, sin_rot, ch_tot)
-    local = lax.all_to_all(spectrum, "chan", split_axis=1, concat_axis=0, tiled=True)
+    latest = lax.psum(1, "chan")
+    back = jnp.stack(jnp.split(spectrum, latest, axis=1), axis=0)
+    finding = lax.all_to_all(back, "chan", 0, 0)
+    local = jnp.concatenate(finding, axis=0)
     group_in = local.shape[0]
     own = local.reshape(group_in, CH_WIN, 2 * frames)
     keep_slots = n_stn // 2 + 1

time: 388 us -> 356 us (0.918)
  local copies, waits for them, and re-layouts: 96.8 us -> 66 us
    unnamed x12 -> x10, local copies, waits for them, and re-layouts: 18.6 us -> 1.39 us
    all_to_all x2 -> x0, local copies, waits for them, and re-layouts: 9.8 us -> none  [per_device(): lax.all_to_all(spectrum, 'chan', split_axis=1, concat_axis=0, tiled=True)]
    reshape x1, local copies, waits for them, and re-layouts: 4.81 us -> 0.02 us  [channelise(): return spectrum.reshape(count, ch_tot, 2, frames)]
  transfers between devices with their start and end apart: 1 -> 1, of which waited for: 1 -> 1; matrix products, arithmetic and copies ran while one was open for 1% -> 2% of each run, Pallas kernels for 0% -> 0%
where the time goes in v1:
time: 356 us; the launch traced here: 355 us
  waiting for transfers between devices  125 us (35%)
  other arithmetic  117 us (33%)
  local copies, waits for them, and re-layouts  66 us (19%)
  matrix products  26.7 us (8%)
  between operations  13.6 us (4%)
  blocking collectives  6.77 us (2%)
    all_gather x1, waiting for transfers between devices, per_device(): lax.all_gather(own, 'stn', axis=0, tiled=True)  125 us
    convert_element_type x1, other arithmetic, twiddles(): sines = jnp.sin(phase).astype(jnp.bfloat16)  35 us
    neg x1, other arithmetic, twiddles(): upper = jnp.concatenate([cosines, -sines], axis=1)  32.4 us
    reshape x1, local copies, waits for them, and re-layouts, correlate(): product = product.reshape(product.shape[0], product.shape[1], 2, rows)  32.3 us
    dot_general x1, matrix products, channelise(): jnp.dot(lhs, table, preferred_element_type=jnp.float32)  13.7 us
    reshape x1, other arithmetic, per_device(): whole = whole.reshape(group_in, 2, CH_WIN, n_stn, group_in)  13.4 us
    dot_general x1, matrix products, correlate(): lax.dot_general(own, rhs, (((2,), (2,)), ((1,), (1,))), preferred_element...  13 us
    gather x1, local copies, waits for them, and re-layouts, per_device(): picked = jnp.take(whole, slot_column, axis=3)  10.9 us
  transfers between devices with their start and end apart: 1, of which 1 were waited for; matrix products, arithmetic and copies ran while one was open for 2% of the time, Pallas kernels for 0%

profile of v1, /device:TPU:2, one launch (start us, length us, event | category | flops | bytes accessed | tf_op | source)
XLA Modules:
  0.0 355.0 jit_solution(14517508592413898480)
XLA Ops:
  6.5 0.0 copy-start.1
  6.5 0.0 all-gather.2.cloned.1.call-start
  6.5 2.4 fusion.33
  8.9 2.1 fusion.45
  11.0 35.0 %sine_convert_fusion = (bf16[8192,256]{1,0:T(8,128)(2,1)}, bf16[8192,256]{1,0:T(8,128)(2,1)}) fusion(), kind=kLoop, calls=%fused_computation.25 | loop fusion | flops 33554432 | bytes 8388608 | tf_op jit(solution)/shard_map/convert_element_type | solution.py:25
  46.0 32.4 %fusion.22 = bf16[8192,256]{1,0:T(8,128)(2,1)} fusion(), kind=kLoop, calls=%fused_computation.34 | loop fusion | flops 37748736 | bytes 4194304 | tf_op jit(solution)/shard_map/neg | solution.py:26
  78.4 0.0 copy-done.1
  78.4 2.1 multiply_add_fusion.1
  80.5 0.2 fusion.52
  80.8 0.2 copy_bitcast_fusion
  81.0 4.4 %add_convert_fusion = (bf16[16,2,2,1,8192]{4,3,2,1,0:T(2,128)(2,1)S(1)}, bf16[16,2,2,1,8192]{4,3,2,1,0:T(2,128)(2,1)S(1)}) fusion(f32[16,8192]{1,0:T(8,128)S(1)} %get-tuple-element.46, f32[2,2,8192]{2,1,0:T(2,128)S(1)} %get-tuple-element.44, f32[16,8192]{1,0:T(8,128)S(1)} %get-tuple-element.47, f32[2,2,8192]{2,1,0:T(2,128)S(1)} %get-tuple-element.45), kind=kLoop, calls=%fused_computation.33 | loop fusion | flops 4194304 | bytes 3407872 | tf_op jit(solution)/shard_map/convert
  85.4 4.8 %pad_maximum_fusion = bf16[16,2,2,2,8192]{4,3,2,1,0:T(2,128)(2,1)S(1)} fusion(bf16[16,2,2,1,8192]{4,3,2,1,0:T(2,128)(2,1)S(1)} %get-tuple-element.21, bf16[16,2,2,1,8192]{4,3,2,1,0:T(2,128)(2,1)S(1)} %get-tuple-element.20), kind=kLoop, calls=%fused_computation.31 | loop fusion | flops 4194304 | bytes 4194304 | tf_op jit(solution)/shard_map/stack | solution.py:53
  90.2 1.2 copy.50
  91.4 13.7 %fusion.26 = bf16[64,512]{1,0:T(8,128)(2,1)S(1)} fusion(bf16[64,16384]{1,0:T(8,128)(2,1)S(1)} %bitcast.49, bf16[8192,256]{1,0:T(8,128)(2,1)} %get-tuple-element.49, bf16[8192,256]{1,0:T(8,128)(2,1)} %get-tuple-element.48, bf16[8192,256]{1,0:T(8,128)(2,1)} %fusion.22), kind=kOutput, calls=%fused_computation.36 | convolution fusion | flops 1140916224 | bytes 14745600 | tf_op jit(solution)/shard_map/dot_general | solution.py:55
  105.2 0.1 pad_maximum_fusion.1
  105.4 6.8 %all_to_all.5 = bf16[4,2,1024,2,2]{2,4,3,1,0:T(2,128)(2,1)S(1)} all-to-all(bf16[4,2,1024,2,2]{2,4,3,1,0:T(2,128)(2,1)S(1)} %pad_maximum_fusion.1), channel_id=1, replica_groups=mesh['stn'=64,'chan'=4] {'chan'}, dimensions={0} | all-to-all | bytes 131072 | tf_op jit(solution)/shard_map/all_to_all | solution.py:92
  112.1 0.7 reshape.355
  112.8 0.0 all-gather.2.cloned.1.call-update
  112.8 0.7 compare_bitcast_fusion
  113.5 0.1 broadcast_in_dim.84
  113.6 0.1 mul.838
  113.7 0.1 copy.33
  113.8 0.1 reduce-window.7
  113.9 0.1 add_reduce_fusion
  114.0 0.7 select_reduce_fusion
  114.7 0.1 broadcast_in_dim.81
  114.8 0.7 broadcast_in_dim.82
  115.5 0.7 fusion.47
  116.2 0.1 broadcast_in_dim.76
  116.3 0.7 broadcast_in_dim.77
  117.0 1.6 copy.41
  118.6 124.9 %all-gather.2.cloned.1.call-done = bf16[512,1024,4]{1,2,0:T(4,128)(2,1)} async-done(((bf16[8,1024,4]{1,2,0:T(4,128)(2,1)}), bf16[512,1024,4]{1,2,0:T(4,128)(2,1)}) %all-gather.2.cloned.1.call-update) | async-done | bytes 4194320 | tf_op jit(solution)/shard_map/all_gather | solution.py:104
  243.5 10.1 %copy.40 = bf16[512,1024,4]{0,2,1:T(4,128)(2,1)} copy(bf16[512,1024,4]{1,2,0:T(4,128)(2,1)} %all-gather.2.cloned.1.call-done) | data formatting | bytes 8388608 | tf_op jit(solution)/shard_map/all_gather | solution.py:104
  253.6 0.0 copy-start
  253.6 7.7 %slice_negate_fusion = (bf16[512,1024,2]{0,2,1:T(2,128)(2,1)S(1)}, bf16[512,1024,2]{0,2,1:T(2,128)(2,1)S(1)}) fusion(bf16[512,1024,4]{0,2,1:T(4,128)(2,1)} %copy.40), kind=kLoop, calls=%fused_computation.30 | loop fusion | flops 1048576 | bytes 8388608 | tf_op jit(solution)/shard_map/neg | solution.py:63
  261.4 0.0 copy-done
  261.4 13.0 %fusion.13 = f32[1024,8,1024]{2,1,0:T(8,128)} fusion(bf16[8,1024,4]{0,2,1:T(4,128)(2,1)S(1)} %copy.41, bf16[512,1024,2]{0,2,1:T(2,128)(2,1)S(1)} %get-tuple-element.19, bf16[512,1024,2]{0,2,1:T(2,128)(2,1)S(1)} %get-tuple-element.18, bf16[512,1024,4]{0,2,1:T(4,128)(2,1)S(1)} %copy-done), kind=kOutput, calls=%fused_computation.19 | convolution fusion | flops 92274688 | bytes 42008576 | tf_op jit(solution)/shard_map/dot_general | solution.py:65
  274.4 32.3 %copy.42 = f32[1024,8,2,512]{0,3,2,1:T(8,128)} copy(f32[1024,8,2,512]{3,1,2,0:T(8,128)} %bitcast.47) | data formatting | bytes 67108864 | tf_op jit(solution)/shard_map/reshape | solution.py:69
  306.6 13.4 %fusion = bf16[8,2,1024,64,8]{2,4,3,1,0:T(8,128)(2,1)S(1)} fusion(f32[1024,8,2,512]{0,3,2,1:T(8,128)} %copy.42, f32[512]{0:T(512)S(1)} %mul.838), kind=kLoop, calls=%fused_computation.2 | loop fusion | flops 16777216 | bytes 50333696 | tf_op jit(solution)/shard_map/reshape | solution.py:106
  320.0 7.0 %copy.43 = bf16[8,2,1024,64,8]{2,4,1,0,3:T(8,128)(2,1)} copy(bf16[8,2,1024,64,8]{2,4,3,1,0:T(8,128)(2,1)S(1)} %fusion) | data formatting | bytes 33554432 | tf_op jit(solution)/shard_map/reshape | solution.py:106
  327.0 0.0 copy-start.2
  327.0 0.0 copy-start.3
  327.0 10.9 %gather_fusion = bf16[33,8,2,1024,8]{3,4,2,1,0:T(8,128)(2,1)} fusion(bf16[8,2,1024,64,8]{2,4,1,0,3:T(8,128)(2,1)} %copy.43, s32[1024]{0:T(1024)S(1)} %pad_clamp_fusion), kind=kCustom, calls=%fused_computation | custom fusion | bytes 17301636 | tf_op jit(solution)/shard_map/jit(_take)/gather | solution.py:107
  337.9 0.0 copy-done.2
  337.9 0.0 copy-done.3
  337.9 10.3 %fusion.9 = bf16[8,2,1024,264]{2,3,1,0:T(8,128)(2,1)} fusion(pred[264]{0:T(512)(128)(4,1)S(1)} %copy-done.2, pred[264]{0:T(512)(128)(4,1)S(1)} %copy-done.3, bf16[33,8,2,1024,8]{3,4,2,1,0:T(8,128)(2,1)} %gather_fusion), kind=kLoop, calls=%fused_computation.15 | loop fusion | flops 8650752 | bytes 17302032 | tf_op jit(solution)/shard_map/jit(_where)/select_n | solution.py:108
  (9 shorter events, 0.2 us)
Async XLA Ops:
  6.5 71.9 %copy-start.1 = (bf16[2,17,2,8192]{3,2,1,0:T(2,128)(2,1)S(1)}, bf16[2,17,2,8192]{3,2,1,0:T(2,128)(2,1)}, u32[]{:S(2)}) copy-start(bf16[2,17,2,8192]{3,2,1,0:T(2,128)(2,1)} %param.2) | copy-start | bytes 3342340
  6.5 237.0 %all-gather.2.cloned.1.call-start = ((), (), s32[]{:S(2)}) async-start(), calls=%async_computation.1 | async-start | bytes 4259840 | tf_op jit(solution)/shard_map/all_gather | solution.py:104
  253.6 7.8 %copy-start = (bf16[512,1024,4]{0,2,1:T(4,128)(2,1)S(1)}, bf16[512,1024,4]{0,2,1:T(4,128)(2,1)}, u32[]{:S(2)}) copy-start(bf16[512,1024,4]{0,2,1:T(4,128)(2,1)} %copy.40) | copy-start | bytes 12582916
  327.0 10.9 %copy-start.2 = (pred[264]{0:T(512)(128)(4,1)S(1)}, pred[264]{0:T(512)(128)(4,1)}, u32[]{:S(2)}) copy-start(pred[264]{0:T(512)(128)(4,1)} %broadcast_in_dim.82) | copy-start | bytes 796
  327.0 10.9 %copy-start.3 = (pred[264]{0:T(512)(128)(4,1)S(1)}, pred[264]{0:T(512)(128)(4,1)}, u32[]{:S(2)}) copy-start(pred[264]{0:T(512)(128)(4,1)} %broadcast_in_dim.77) | copy-start | bytes 796
Sparse Core Ops, SparseCore 0:
  112.9 130.5 all-gather.1
